TPU v7x, 32 devices: a whole 2x2x4 slice. The times are simulated.
32 devices in a mesh: groups: 2 (over y), row: 4 (over z), col: 4 (over x, core).
Axes of the slice: x: 2, y: 2, z: 4, core: 2. Of those that a mesh axis runs over, the one named last changes fastest.
Arguments:
- row_embed: bfloat16 [8, 256, 1024], P(('groups', 'row'), 'col'), parts along dimension 0, may hold values from -6 to 6
- col_embed: bfloat16 [8, 256, 1024], P(('groups', 'col'), 'row'), parts along dimension 0, may hold values from -6 to 6
- pos_rows: int32 [8, 4, 256], P(('groups', 'row'), 'col'), parts along dimension 0, may hold values from 0 to 255
- pos_cols: int32 [8, 4, 256], P(('groups', 'row'), 'col'), parts along dimension 0, may hold values from 0 to 255
- logit_scale: float32 [1], replicated, may hold values from 0.06 to 0.1
- logit_bias: float32 [1], replicated, may hold values from -9 to -7
Outputs:
- logits: bfloat16 [2048, 1024], P(('groups', 'row'), 'col'), parts along dimension 0
- row_grad: bfloat16 [8, 256, 1024], P(('groups', 'row'), 'col'), parts along dimension 0
- col_grad: bfloat16 [8, 256, 1024], P(('groups', 'col'), 'row'), parts along dimension 0
There are 2 independent parts, one for each index of `groups`. A program takes and returns all parts, laid end to end along the dimension named above; an argument that names none is the same for every part. Nothing has to cross between parts.
Inputs may be any that keep to these rules, and one draw needn't show every extreme that they name: `pos_rows`: indices are local to the tile; a pair listed twice counts once. `pos_cols`: indices are local to the tile and match pos_rows entry by entry.
All inputs are finite; a program needn't handle non-finite values.
Results may differ from a plain program's by a relative error of at most 0.012.
Values may be sent and summed in bfloat16 or wider, within the bound.
A program may use at most 64 MiB of HBM per device.

v0:
```python
import jax
import jax.numpy as jnp
from jax import lax
from jax.sharding import PartitionSpec as P


def local(row_embed, col_embed, pos_rows, pos_cols, logit_scale, logit_bias):
    factor = logit_scale[0]
    offset = logit_bias[0]
    row_block = lax.all_gather(row_embed, "col", axis=1, tiled=True)[0]
    rows_tile = row_block.shape[0]
    cols_tile = col_embed.shape[1] * lax.axis_size("row")
    labels = jnp.zeros((rows_tile, cols_tile), jnp.float32)
    labels = labels.at[pos_rows[0, 0], pos_cols[0, 0]].max(1.0)
    col_block = lax.all_gather(col_embed, "row", axis=1, tiled=True)[0]
    scores = (
        factor * jnp.einsum("rd,jd->rj", row_block, col_block, preferred_element_type=jnp.float32)
        + offset
    )
    grad_tile = (jax.nn.sigmoid(scores) - labels).astype(jnp.bfloat16)
    logit_tile = scores.astype(jnp.bfloat16)
    row_sum = lax.psum_scatter(
        jnp.dot(grad_tile, col_block, preferred_element_type=jnp.float32).astype(jnp.bfloat16),
        "col",
        scatter_dimension=0,
        tiled=True,
    ).astype(jnp.float32)
    col_sum = lax.psum_scatter(
        lax.dot_general(
            grad_tile, row_block, (((0,), (0,)), ((), ())), preferred_element_type=jnp.float32
        ).astype(jnp.bfloat16),
        "row",
        scatter_dimension=0,
        tiled=True,
    ).astype(jnp.float32)
    row_grad = (factor * row_sum).astype(jnp.bfloat16)[None]
    col_grad = (factor * col_sum).astype(jnp.bfloat16)[None]
    return (logit_tile, row_grad, col_grad)


def solution(mesh):
    in_specs = (
        P(("groups", "row"), "col", None),
        P(("groups", "col"), "row", None),
        P(("groups", "row"), "col", None),
        P(("groups", "row"), "col", None),
        P(),
        P(),
    )
    out_specs = (
        P(("groups", "row"), "col"),
        P(("groups", "row"), "col", None),
        P(("groups", "col"), "row", None),
    )
    return jax.shard_map(local, mesh=mesh, in_specs=in_specs, out_specs=out_specs, check_vma=False)
```

profile of v0, /device:TPU:0, one launch (start us, length us, event | category | flops | bytes accessed | tf_op | source)
XLA Modules:
  0.0 104.1 jit_solution(3557589187182137713)
XLA Ops:
  7.2 0.0 reduce-scatter.3.cloned.1.call-start
  8.5 0.0 copy-start
  8.5 9.0 %all_gather.6 = bf16[1,256,1024]{2,1,0:T(8,128)(2,1)S(1)} all-gather(bf16[1,64,1024]{2,1,0:T(8,128)(2,1)} %param.6), channel_id=1, replica_groups=mesh['groups'=2,'row'=4,'col'=4] {'col'}, dimensions={1}, use_global_device_ids=true | all-gather | bytes 655360 | tf_op jit(solution)/shard_map/all_gather | solution.py:10
  17.5 0.0 copy-done
  17.5 0.0 copy-start.1
  17.5 0.0 copy-start.2
  17.5 16.5 %all_gather.7 = bf16[1,256,1024]{2,1,0:T(8,128)(2,1)S(1)} all-gather(bf16[1,64,1024]{2,1,0:T(8,128)(2,1)S(1)} %copy-done), channel_id=1, replica_groups=mesh['groups'=2,'row'=4,'col'=4] {'row'}, dimensions={1}, use_global_device_ids=true | all-gather | bytes 655360 | tf_op jit(solution)/shard_map/all_gather | solution.py:15
  34.0 0.0 copy-done.1
  34.0 0.0 copy-done.2
  34.0 12.7 %scatter_fusion = f32[256,256]{1,0:T(8,128)S(1)} fusion(f32[256,256]{1,0:T(8,128)S(1)} %broadcast_in_dim.14, s32[256]{0:T(256)S(1)} %bitcast.31, f32[256]{0:T(256)S(1)} %broadcast.56), kind=kCustom, calls=%fused_computation | custom fusion | flops 256 | bytes 5120 | tf_op jit(solution)/shard_map/scatter-max | solution.py:14
  46.7 1.0 subtract_convert_fusion
  47.8 1.1 %convolution_convert_fusion.1 = bf16[256,1024]{1,0:T(8,128)(2,1)} fusion(bf16[256,256]{1,0:T(8,128)(2,1)S(1)} %get-tuple-element.3, bf16[1,256,1024]{2,1,0:T(8,128)(2,1)S(1)} %all_gather.7), kind=kOutput, calls=%fused_computation.2 | convolution fusion | flops 134479872 | bytes 1179648 | tf_op jit(solution)/shard_map/dot_general | solution.py:23
  48.8 0.0 reduce-scatter.3.cloned.1.call-update
  48.9 0.0 reduce-scatter.5.cloned.1.call-start
  48.9 1.1 %convolution_convert_fusion = bf16[256,1024]{1,0:T(8,128)(2,1)} fusion(bf16[256,256]{1,0:T(8,128)(2,1)S(1)} %get-tuple-element.3, bf16[1,256,1024]{2,1,0:T(8,128)(2,1)S(1)} %all_gather.6), kind=kOutput, calls=%fused_computation.1 | convolution fusion | flops 134479872 | bytes 1179648 | tf_op jit(solution)/shard_map/dot_general | solution.py:29
  50.0 0.0 reduce-scatter.5.cloned.1.call-update
  50.1 21.6 %reduce-scatter.3.cloned.1.call-done = bf16[64,1024]{1,0:T(8,128)(2,1)} async-done(((bf16[256,1024]{1,0:T(8,128)(2,1)}), bf16[64,1024]{1,0:T(8,128)(2,1)}) %reduce-scatter.3.cloned.1.call-update) | async-done | bytes 131088 | tf_op jit(solution)/shard_map/reduce_scatter | solution.py:22
  71.6 1.6 %fusion.5 = bf16[1,64,1024]{2,1,0:T(8,128)(2,1)} fusion(bf16[64,1024]{1,0:T(8,128)(2,1)} %reduce-scatter.3.cloned.1.call-done, f32[]{:T(128)} %bitcast.28), kind=kLoop, calls=%fused_computation.12 | loop fusion | flops 196608 | bytes 262148 | tf_op jit(solution)/shard_map/broadcast_in_dim | solution.py:36
  73.2 22.5 %reduce-scatter.5.cloned.1.call-done = bf16[64,1024]{1,0:T(8,128)(2,1)} async-done(((bf16[256,1024]{1,0:T(8,128)(2,1)}), bf16[64,1024]{1,0:T(8,128)(2,1)}) %reduce-scatter.5.cloned.1.call-update) | async-done | bytes 131088 | tf_op jit(solution)/shard_map/reduce_scatter | solution.py:28
  95.7 1.6 %fusion.6 = bf16[1,64,1024]{2,1,0:T(8,128)(2,1)} fusion(bf16[64,1024]{1,0:T(8,128)(2,1)} %reduce-scatter.5.cloned.1.call-done, f32[]{:T(128)} %bitcast.29), kind=kLoop, calls=%fused_computation.13 | loop fusion | flops 196608 | bytes 262148 | tf_op jit(solution)/shard_map/broadcast_in_dim | solution.py:37
  (3 shorter events, 0.0 us)
Async XLA Ops:
  7.2 64.5 %reduce-scatter.3.cloned.1.call-start = ((), (), s32[]{:S(2)}) async-start(), calls=%async_computation.2 | async-start | bytes 655360 | tf_op jit(solution)/shard_map/reduce_scatter | solution.py:22
  8.5 9.0 %copy-start = (bf16[1,64,1024]{2,1,0:T(8,128)(2,1)S(1)}, bf16[1,64,1024]{2,1,0:T(8,128)(2,1)}, u32[]{:S(2)}) copy-start(bf16[1,64,1024]{2,1,0:T(8,128)(2,1)} %param.7) | copy-start | bytes 393220
  17.5 16.5 %copy-start.1 = (s32[1,1,256]{2,1,0:T(1,128)S(1)}, s32[1,1,256]{2,1,0:T(1,128)}, u32[]{:S(2)}) copy-start(s32[1,1,256]{2,1,0:T(1,128)} %param.9) | copy-start | bytes 3076
  17.5 16.5 %copy-start.2 = (s32[1,1,256]{2,1,0:T(1,128)S(1)}, s32[1,1,256]{2,1,0:T(1,128)}, u32[]{:S(2)}) copy-start(s32[1,1,256]{2,1,0:T(1,128)} %param.8) | copy-start | bytes 3076
  48.9 46.9 %reduce-scatter.5.cloned.1.call-start = ((), (), s32[]{:S(2)}) async-start(), calls=%async_computation.3 | async-start | bytes 655360 | tf_op jit(solution)/shard_map/reduce_scatter | solution.py:28
Sparse Core Ops, SparseCore 0:
  49.0 22.6 reduce-scatter.2
  74.0 21.6 reduce-scatter.4
where the time goes:
time: 104 us
  waiting for transfers between devices  44.1 us (42%)
  blocking collectives  25.4 us (24%)
  other arithmetic  15.9 us (15%)
  between operations  15.4 us (15%)
  matrix products  3.21 us (3%)
    reduce_scatter x1, waiting for transfers between devices, local(): lax.psum_scatter(lax.dot_general(grad_tile, row_block, (((0,), (0,)), (()...  22.5 us
    reduce_scatter x1, waiting for transfers between devices, local(): lax.psum_scatter(jnp.dot(grad_tile, col_block, preferred_element_type=jnp...  21.6 us
    all_gather x1, blocking collectives, local(): col_block = lax.all_gather(col_embed, 'row', axis=1, tiled=True)[0]  16.5 us
    another operation x1, other arithmetic, local(): labels = labels.at[pos_rows[0, 0], pos_cols[0, 0]].max(1.0)  12.7 us
    all_gather x1, blocking collectives, local(): row_block = lax.all_gather(row_embed, 'col', axis=1, tiled=True)[0]  8.96 us
  transfers between devices with their start and end apart: 2, of which 2 were waited for; matrix products, arithmetic and copies ran while one was open for 3% of the time, Pallas kernels for 0%

commit v1 on v0

v1 whole, which is shorter than its diff:
```python
import functools

import jax
import jax.numpy as jnp
from jax import lax
from jax.experimental import pallas as pl
from jax.experimental.pallas import tpu as pltpu
from jax.sharding import PartitionSpec as P

NT = (((1,), (1,)), ((), ()))


def nearest(me, n, step):
    inner = jnp.minimum(me, n - 1 - me)
    both = (step + 1) // 2 * (2 * (step % 2) - 1)
    one = (step - inner) * jnp.where(2 * me < n, 1, -1)
    return me + jnp.where(step <= 2 * inner, both, one)


def kernel(
    nr, nc, scale_ref, bias_ref, pr_ref, pc_ref, row_ref, col_ref,
    logit_out, row_out, col_out,
    rows, cols, labels, lt, gt, logit_v, cp, cp_in, rp, rp_in, row_v, col_v,
    own_sem, out_sem, row_send, row_recv, col_send, col_recv, cp_send, cp_recv, rp_send, rp_recv,
):
    g, r, c = lax.axis_index("groups"), lax.axis_index("row"), lax.axis_index("col")
    rs, cs = row_ref.shape[1], col_ref.shape[1]
    depth = row_ref.shape[2]
    rows_tile, cols_tile = rs * nc, cs * nr

    barrier = pltpu.get_barrier_semaphore()
    for k in range(1, nr):
        pl.semaphore_signal(barrier, inc=1, device_id=(g, lax.rem(r + k, nr), c), device_id_type=pl.DeviceIdType.MESH)
    for k in range(1, nc):
        pl.semaphore_signal(barrier, inc=1, device_id=(g, r, lax.rem(c + k, nc)), device_id_type=pl.DeviceIdType.MESH)
    own_row = pltpu.make_async_copy(row_ref.at[0], rows.at[c], own_sem.at[0])
    own_col = pltpu.make_async_copy(col_ref.at[0], cols.at[r], own_sem.at[1])
    own_row.start()
    own_col.start()

    def remote(src, dst, send, recv, where):
        return pltpu.make_async_remote_copy(
            src_ref=src, dst_ref=dst, send_sem=send, recv_sem=recv, device_id=where, device_id_type=pl.DeviceIdType.MESH
        )

    def row_copy(k, slot):
        return remote(row_ref.at[0], rows.at[slot], row_send.at[k], row_recv.at[slot], (g, r, lax.rem(c + k, nc)))

    def col_copy(peer, slot):
        return remote(col_ref.at[0], cols.at[slot], col_send.at[peer], col_recv.at[slot], (g, peer, c))

    def cp_copy(peer, slot):
        return remote(cp.at[peer], cp_in.at[slot], cp_send.at[peer], cp_recv.at[slot], (g, peer, c))

    def rp_copy(peer, slot):
        return remote(rp.at[peer], rp_in.at[slot], rp_send.at[peer], rp_recv.at[slot], (g, r, peer))

    pl.semaphore_wait(barrier, nr + nc - 2)
    for k in range(1, nr):
        col_copy(nearest(r, nr, k), r).start()
    for k in range(1, nc):
        row_copy(k, c).start()

    factor, offset = scale_ref[0], bias_ref[0]
    pairs = pr_ref.shape[2]
    hit_rows = (lax.broadcasted_iota(jnp.int32, (rows_tile, pairs), 0) == pr_ref[0]).astype(jnp.bfloat16)
    hit_cols = (lax.broadcasted_iota(jnp.int32, (cols_tile, pairs), 0) == pc_ref[0]).astype(jnp.bfloat16)
    count = lax.dot_general(hit_cols, hit_rows, NT, preferred_element_type=jnp.float32)
    labels[...] = jnp.where(count > 0.5, 1.0, 0.0)

    own_row.wait()
    own_col.wait()
    for k in range(1, nc):
        row_copy(k, lax.rem(c + k, nc)).wait_recv()

    def block(s):
        at = pl.ds(pl.multiple_of(s * cs, cs), cs)
        row_all = rows[...].reshape(rows_tile, depth)
        scores = factor * lax.dot_general(cols[s], row_all, NT, preferred_element_type=jnp.float32) + offset
        lt[at, :] = scores
        grad = (jax.nn.sigmoid(scores) - labels[at, :]).astype(jnp.bfloat16)
        gt[at, :] = grad
        return jnp.dot(grad, row_all, preferred_element_type=jnp.float32).astype(jnp.bfloat16)

    cp_in[r] = block(r)

    def arrived(k):
        s = nearest(r, nr, k)
        col_copy(s, s).wait_recv()
        cp[s] = block(s)
        cp_copy(s, r).start()

    if nr <= 4:
        for k in range(1, nr):
            arrived(k)
    else:
        pl.loop(1, nr)(arrived)

    cols_all = cols[...].reshape(cols_tile, depth)
    grad = gt[...].T
    out = jnp.dot(grad, cols_all, preferred_element_type=jnp.float32).astype(jnp.bfloat16)
    rp[...] = out.reshape(nc, rs, depth)
    for k in range(1, nc):
        rp_copy(lax.rem(c + k, nc), c).start()
    rp_in[c] = rp[c]
    logit_v[...] = lt[...].T.astype(jnp.bfloat16)
    logit_copy = pltpu.make_async_copy(logit_v, logit_out, out_sem.at[0])
    logit_copy.start()

    def total(parts, n):
        add = parts[0].astype(jnp.float32)
        for s in range(1, n):
            add += parts[s].astype(jnp.float32)
        return (factor * add).astype(jnp.bfloat16)

    for k in range(1, nr):
        s = nearest(r, nr, k)
        cp_copy(s, s).wait_recv()
    col_v[...] = total(cp_in, nr)
    col_done = pltpu.make_async_copy(col_v, col_out.at[0], out_sem.at[1])
    col_done.start()
    for k in range(1, nc):
        s = lax.rem(c + k, nc)
        rp_copy(s, s).wait_recv()
    row_v[...] = total(rp_in, nc)
    row_done = pltpu.make_async_copy(row_v, row_out.at[0], out_sem.at[2])
    row_done.start()

    for k in range(1, nr):
        s = nearest(r, nr, k)
        col_copy(s, r).wait_send()
        cp_copy(s, r).wait_send()
    for k in range(1, nc):
        row_copy(k, c).wait_send()
        rp_copy(lax.rem(c + k, nc), c).wait_send()
    logit_copy.wait()
    col_done.wait()
    row_done.wait()


def local(nr, nc, row_embed, col_embed, pos_rows, pos_cols, logit_scale, logit_bias):
    _, rs, depth = row_embed.shape
    cs = col_embed.shape[1]
    rows_tile, cols_tile = rs * nc, cs * nr
    bf16, f32 = jnp.bfloat16, jnp.float32
    smem, vmem, hbm = (pl.BlockSpec(memory_space=m) for m in (pltpu.SMEM, pltpu.VMEM, pl.ANY))
    dma = pltpu.SemaphoreType.DMA
    return pl.pallas_call(
        functools.partial(kernel, nr, nc),
        out_shape=(
            jax.ShapeDtypeStruct((rows_tile, cols_tile), bf16),
            jax.ShapeDtypeStruct((1, rs, depth), bf16),
            jax.ShapeDtypeStruct((1, cs, depth), bf16),
        ),
        in_specs=[smem, smem, vmem, vmem, hbm, hbm],
        out_specs=(hbm, hbm, hbm),
        scratch_shapes=[
            pltpu.VMEM((nc, rs, depth), bf16),
            pltpu.VMEM((nr, cs, depth), bf16),
            pltpu.VMEM((cols_tile, rows_tile), f32),
            pltpu.VMEM((cols_tile, rows_tile), f32),
            pltpu.VMEM((cols_tile, rows_tile), bf16),
            pltpu.VMEM((rows_tile, cols_tile), bf16),
            pltpu.VMEM((nr, cs, depth), bf16),
            pltpu.VMEM((nr, cs, depth), bf16),
            pltpu.VMEM((nc, rs, depth), bf16),
            pltpu.VMEM((nc, rs, depth), bf16),
            pltpu.VMEM((rs, depth), bf16),
            pltpu.VMEM((cs, depth), bf16),
            dma((2,)),
            dma((3,)),
            dma((nc,)),
            dma((nc,)),
            dma((nr,)),
            dma((nr,)),
            dma((nr,)),
            dma((nr,)),
            dma((nc,)),
            dma((nc,)),
        ],
        compiler_params=pltpu.CompilerParams(
            collective_id=0, has_side_effects=True, vmem_limit_bytes=50 * 1024 * 1024
        ),
    )(logit_scale, logit_bias, pos_rows, pos_cols, row_embed, col_embed)


def solution(mesh):
    in_specs = (
        P(("groups", "row"), "col", None),
        P(("groups", "col"), "row", None),
        P(("groups", "row"), "col", None),
        P(("groups", "row"), "col", None),
        P(),
        P(),
    )
    out_specs = (
        P(("groups", "row"), "col"),
        P(("groups", "row"), "col", None),
        P(("groups", "col"), "row", None),
    )
    body = functools.partial(local, mesh.shape["row"], mesh.shape["col"])
    return jax.shard_map(body, mesh=mesh, in_specs=in_specs, out_specs=out_specs, check_vma=False)
```

time: 104 us -> 35.9 us (0.35)
  waiting for transfers between devices: 44.1 us -> 0 us
  Pallas kernels: 0 us -> 30 us
  blocking collectives: 25.4 us -> 0 us
  other arithmetic: 15.9 us -> 0 us
  between operations: 15.4 us -> 2 us
  local copies, waits for them, and re-layouts: 0.03 us -> 3.78 us
  matrix products: 3.21 us -> 0 us
    reduce_scatter x2 -> x0, waiting for transfers between devices: 44.1 us -> none  [the longest x1 22.5 us: local(): lax.psum_scatter(lax.dot_general(grad_tile, row_block, (((0,), (0,)), (()...]
    pallas_call x0 -> x1, Pallas kernels: none -> 30 us  [local(): pl.pallas_call(functools.partial(kernel, nr, nc), out_shape=(jax.ShapeDty...]
    all_gather x2 -> x0, blocking collectives: 25.4 us -> none  [the longest x1 16.5 us: local(): col_block = lax.all_gather(col_embed, 'row', axis=1, tiled=True)[0]]
    another operation x1 -> x0, other arithmetic: 12.7 us -> none  [local(): labels = labels.at[pos_rows[0, 0], pos_cols[0, 0]].max(1.0)]
    unnamed x6 -> x11, local copies, waits for them, and re-layouts: 0.01 us -> 3.78 us
    dot_general x3 -> x0, matrix products: 3.21 us -> none  [the longest x1 1.11 us: local(): lax.dot_general(grad_tile, row_block, (((0,), (0,)), ((), ())), preferred...]
    broadcast_in_dim x2 -> x0, other arithmetic: 3.16 us -> none  [the longest x1 1.58 us: local(): row_grad = (factor * row_sum).astype(jnp.bfloat16)[None]]
  transfers between devices with their start and end apart: 2 -> 0, of which waited for: 2 -> 0; matrix products, arithmetic and copies ran while one was open for 3% -> 0% of each run, Pallas kernels for 0% -> 0%
where the time goes in v1:
time: 35.9 us; the launch traced here: 35.7 us
  Pallas kernels  30 us (84%)
  local copies, waits for them, and re-layouts  3.78 us (11%)
  between operations  2 us (6%)
    pallas_call x1, Pallas kernels, local(): pl.pallas_call(functools.partial(kernel, nr, nc), out_shape=(jax.ShapeDty...  30 us
    unnamed x11, local copies, waits for them, and re-layouts  3.78 us

profile of v1, /device:TPU:0, one launch (start us, length us, event | category | flops | bytes accessed | tf_op | source)
XLA Modules:
  0.0 35.7 jit_solution(14374341599393894582)
XLA Ops:
  0.6 0.0 copy-start.3
  1.3 0.0 copy-start.2
  2.0 0.0 copy-done.3
  2.0 0.0 copy-done.2
  2.0 0.0 copy-start
  2.0 0.9 %copy-done = bf16[1,64,1024]{2,1,0:T(8,128)(2,1)S(1)} copy-done((bf16[1,64,1024]{2,1,0:T(8,128)(2,1)S(1)}, bf16[1,64,1024]{2,1,0:T(8,128)(2,1)}, u32[]{:S(2)}) %copy-start) | copy-done | bytes 131096
  2.9 0.0 copy-start.1
  2.9 0.9 %copy-done.1 = bf16[1,64,1024]{2,1,0:T(8,128)(2,1)S(1)} copy-done((bf16[1,64,1024]{2,1,0:T(8,128)(2,1)S(1)}, bf16[1,64,1024]{2,1,0:T(8,128)(2,1)}, u32[]{:S(2)}) %copy-start.1) | copy-done | bytes 131096
  3.8 30.0 %shard_map.85 = (bf16[256,256]{1,0:T(8,128)(2,1)S(1)}, bf16[1,64,1024]{2,1,0:T(8,128)(2,1)S(1)}, bf16[1,64,1024]{2,1,0:T(8,128)(2,1)S(1)}) custom-call(f32[1]{0:T(128)S(6)} %copy.12.scale_ref, f32[1]{0:T(128)S(6)} %copy.13.bias_ref, s32[1,1,256]{2,1,0:T(1,128)S(1)} %copy-done.2, s32[1,1,256]{2,1,0:T(1,128)S(1)} %copy-done.3, ...), custom_call_target="tpu_custom_call" | custom-call | tf_op jit(solution)/shard_map/pallas_call | solution.py:148
  33.8 0.7 %copy.14 = bf16[256,256]{1,0:T(8,128)(2,1)} copy(bf16[256,256]{1,0:T(8,128)(2,1)S(1)} %get-tuple-element.6) | data formatting | bytes 262144
  34.4 0.7 %copy.15 = bf16[1,64,1024]{2,1,0:T(8,128)(2,1)} copy(bf16[1,64,1024]{2,1,0:T(8,128)(2,1)S(1)} %get-tuple-element.7) | data formatting | bytes 262144
  35.1 0.7 %copy.16 = bf16[1,64,1024]{2,1,0:T(8,128)(2,1)} copy(bf16[1,64,1024]{2,1,0:T(8,128)(2,1)S(1)} %get-tuple-element.8) | data formatting | bytes 262144
Async XLA Ops:
  0.6 1.3 %copy-start.3 = (s32[1,1,256]{2,1,0:T(1,128)S(1)}, s32[1,1,256]{2,1,0:T(1,128)}, u32[]{:S(2)}) copy-start(s32[1,1,256]{2,1,0:T(1,128)} %pc_ref.1) | copy-start | bytes 3076
  1.3 0.7 %copy-start.2 = (s32[1,1,256]{2,1,0:T(1,128)S(1)}, s32[1,1,256]{2,1,0:T(1,128)}, u32[]{:S(2)}) copy-start(s32[1,1,256]{2,1,0:T(1,128)} %pr_ref.1) | copy-start | bytes 3076
  2.0 0.9 %copy-start = (bf16[1,64,1024]{2,1,0:T(8,128)(2,1)S(1)}, bf16[1,64,1024]{2,1,0:T(8,128)(2,1)}, u32[]{:S(2)}) copy-start(bf16[1,64,1024]{2,1,0:T(8,128)(2,1)} %row_ref.1) | copy-start | bytes 393220
  2.9 0.9 %copy-start.1 = (bf16[1,64,1024]{2,1,0:T(8,128)(2,1)S(1)}, bf16[1,64,1024]{2,1,0:T(8,128)(2,1)}, u32[]{:S(2)}) copy-start(bf16[1,64,1024]{2,1,0:T(8,128)(2,1)} %col_ref.1) | copy-start | bytes 393220

commit v2 on v1

--- a/solution.py
+++ b/solution.py
@@ -18,10 +18,10 @@
 
 
 def kernel(
-    nr, nc, scale_ref, bias_ref, pr_ref, pc_ref, row_ref, col_ref,
+    nr, nc, scale_hbm, bias_hbm, pr_hbm, pc_hbm, row_ref, col_ref,
     logit_out, row_out, col_out,
-    rows, cols, labels, lt, gt, logit_v, cp, cp_in, rp, rp_in, row_v, col_v,
-    own_sem, out_sem, row_send, row_recv, col_send, col_recv, cp_send, cp_recv, rp_send, rp_recv,
+    scale_ref, bias_ref, pr_ref, pc_ref, rows, cols, labels, lt, gt, cp, cp_in, rp, rp_in,
+    own_sem, row_send, row_recv, col_send, col_recv, cp_send, cp_recv, rp_send, rp_recv,
 ):
     g, r, c = lax.axis_index("groups"), lax.axis_index("row"), lax.axis_index("col")
     rs, cs = row_ref.shape[1], col_ref.shape[1]
@@ -35,8 +35,14 @@
         pl.semaphore_signal(barrier, inc=1, device_id=(g, r, lax.rem(c + k, nc)), device_id_type=pl.DeviceIdType.MESH)
     own_row = pltpu.make_async_copy(row_ref.at[0], rows.at[c], own_sem.at[0])
     own_col = pltpu.make_async_copy(col_ref.at[0], cols.at[r], own_sem.at[1])
-    own_row.start()
-    own_col.start()
+    small = [
+        pltpu.make_async_copy(src, dst, own_sem.at[2 + i])
+        for i, (src, dst) in enumerate(
+            ((pr_hbm, pr_ref), (pc_hbm, pc_ref), (scale_hbm, scale_ref), (bias_hbm, bias_ref))
+        )
+    ]
+    for copy in [*small, own_row, own_col]:
+        copy.start()
 
     def remote(src, dst, send, recv, where):
         return pltpu.make_async_remote_copy(
@@ -61,6 +67,8 @@
     for k in range(1, nc):
         row_copy(k, c).start()
 
+    for copy in small:
+        copy.wait()
     factor, offset = scale_ref[0], bias_ref[0]
     pairs = pr_ref.shape[2]
     hit_rows = (lax.broadcasted_iota(jnp.int32, (rows_tile, pairs), 0) == pr_ref[0]).astype(jnp.bfloat16)
@@ -103,9 +111,7 @@
     for k in range(1, nc):
         rp_copy(lax.rem(c + k, nc), c).start()
     rp_in[c] = rp[c]
-    logit_v[...] = lt[...].T.astype(jnp.bfloat16)
-    logit_copy = pltpu.make_async_copy(logit_v, logit_out, out_sem.at[0])
-    logit_copy.start()
+    logit_out[...] = lt[...].T.astype(jnp.bfloat16)
 
     def total(parts, n):
         add = parts[0].astype(jnp.float32)
@@ -116,15 +122,11 @@
     for k in range(1, nr):
         s = nearest(r, nr, k)
         cp_copy(s, s).wait_recv()
-    col_v[...] = total(cp_in, nr)
-    col_done = pltpu.make_async_copy(col_v, col_out.at[0], out_sem.at[1])
-    col_done.start()
+    col_out[0] = total(cp_in, nr)
     for k in range(1, nc):
         s = lax.rem(c + k, nc)
         rp_copy(s, s).wait_recv()
-    row_v[...] = total(rp_in, nc)
-    row_done = pltpu.make_async_copy(row_v, row_out.at[0], out_sem.at[2])
-    row_done.start()
+    row_out[0] = total(rp_in, nc)
 
     for k in range(1, nr):
         s = nearest(r, nr, k)
@@ -133,9 +135,16 @@
     for k in range(1, nc):
         row_copy(k, c).wait_send()
         rp_copy(lax.rem(c + k, nc), c).wait_send()
-    logit_copy.wait()
-    col_done.wait()
-    row_done.wait()
+
+
+def write_out(*refs):
+    sems = refs[-1]
+    held, out = refs[:3], refs[3:6]
+    copies = [pltpu.make_async_copy(src, dst, sems.at[i]) for i, (src, dst) in enumerate(zip(held, out))]
+    for copy in copies:
+        copy.start()
+    for copy in copies:
+        copy.wait()
 
 
 def local(nr, nc, row_embed, col_embed, pos_rows, pos_cols, logit_scale, logit_bias):
@@ -143,32 +152,35 @@
     cs = col_embed.shape[1]
     rows_tile, cols_tile = rs * nc, cs * nr
     bf16, f32 = jnp.bfloat16, jnp.float32
-    smem, vmem, hbm = (pl.BlockSpec(memory_space=m) for m in (pltpu.SMEM, pltpu.VMEM, pl.ANY))
+    vmem, hbm = (pl.BlockSpec(memory_space=m) for m in (pltpu.VMEM, pltpu.HBM))
     dma = pltpu.SemaphoreType.DMA
-    return pl.pallas_call(
+    shapes = (
+        jax.ShapeDtypeStruct((rows_tile, cols_tile), bf16),
+        jax.ShapeDtypeStruct((1, rs, depth), bf16),
+        jax.ShapeDtypeStruct((1, cs, depth), bf16),
+    )
+    operands = (pos_rows, pos_cols, row_embed, col_embed)
+    pinned = [pltpu.with_memory_space_constraint(x, pltpu.HBM) for x in operands]
+    held = pl.pallas_call(
         functools.partial(kernel, nr, nc),
-        out_shape=(
-            jax.ShapeDtypeStruct((rows_tile, cols_tile), bf16),
-            jax.ShapeDtypeStruct((1, rs, depth), bf16),
-            jax.ShapeDtypeStruct((1, cs, depth), bf16),
-        ),
-        in_specs=[smem, smem, vmem, vmem, hbm, hbm],
-        out_specs=(hbm, hbm, hbm),
+        out_shape=shapes,
+        in_specs=[hbm] * 6,
+        out_specs=(vmem,) * 3,
         scratch_shapes=[
+            pltpu.SMEM((1,), f32),
+            pltpu.SMEM((1,), f32),
+            pltpu.VMEM(pos_rows.shape, jnp.int32),
+            pltpu.VMEM(pos_cols.shape, jnp.int32),
             pltpu.VMEM((nc, rs, depth), bf16),
             pltpu.VMEM((nr, cs, depth), bf16),
             pltpu.VMEM((cols_tile, rows_tile), f32),
             pltpu.VMEM((cols_tile, rows_tile), f32),
             pltpu.VMEM((cols_tile, rows_tile), bf16),
-            pltpu.VMEM((rows_tile, cols_tile), bf16),
             pltpu.VMEM((nr, cs, depth), bf16),
             pltpu.VMEM((nr, cs, depth), bf16),
             pltpu.VMEM((nc, rs, depth), bf16),
             pltpu.VMEM((nc, rs, depth), bf16),
-            pltpu.VMEM((rs, depth), bf16),
-            pltpu.VMEM((cs, depth), bf16),
-            dma((2,)),
-            dma((3,)),
+            dma((6,)),
             dma((nc,)),
             dma((nc,)),
             dma((nr,)),
@@ -181,7 +193,14 @@
         compiler_params=pltpu.CompilerParams(
             collective_id=0, has_side_effects=True, vmem_limit_bytes=50 * 1024 * 1024
         ),
-    )(logit_scale, logit_bias, pos_rows, pos_cols, row_embed, col_embed)
+    )(logit_scale, logit_bias, *pinned)
+    return pl.pallas_call(
+        write_out,
+        out_shape=shapes,
+        in_specs=[vmem] * 3,
+        out_specs=(hbm,) * 3,
+        scratch_shapes=[dma((3,))],
+    )(*held)
 
 
 def solution(mesh):

time: 35.9 us -> 35.7 us (level)
  local copies, waits for them, and re-layouts: 3.78 us -> 1.92 us
  Pallas kernels: 30 us -> 31.7 us
    unnamed x11 -> x6, local copies, waits for them, and re-layouts: 3.78 us -> 1.92 us
    pallas_call x1 -> x2, Pallas kernels: 30 us -> 31.7 us  [the longest x1 29.9 us: local(): pl.pallas_call(functools.partial(kernel, nr, nc), out_shape=shapes, in_sp...]
where the time goes in v2:
time: 35.7 us; the launch traced here: 35.5 us
  Pallas kernels  31.7 us (89%)
  between operations  1.94 us (5%)
  local copies, waits for them, and re-layouts  1.92 us (5%)
    pallas_call x1, Pallas kernels, local(): pl.pallas_call(functools.partial(kernel, nr, nc), out_shape=shapes, in_sp...  29.9 us
    unnamed x6, local copies, waits for them, and re-layouts  1.92 us
    pallas_call x1, Pallas kernels, local(): pl.pallas_call(write_out, out_shape=shapes, in_specs=[vmem] * 3, out_spec...  1.79 us

profile of v2, /device:TPU:0, one launch (start us, length us, event | category | flops | bytes accessed | tf_op | source)
XLA Modules:
  0.0 35.5 jit_solution(6685969870997266728)
XLA Ops:
  1.9 29.9 %shard_map.85 = (bf16[256,256]{1,0:T(8,128)(2,1)S(1)}, bf16[1,64,1024]{2,1,0:T(8,128)(2,1)S(1)}, bf16[1,64,1024]{2,1,0:T(8,128)(2,1)S(1)}) custom-call(f32[1]{0:T(128)S(6)} %copy.9.scale_hbm, f32[1]{0:T(128)S(6)} %copy.10.bias_hbm, s32[1,1,256]{2,1,0:T(1,128)} %pr_hbm.1, s32[1,1,256]{2,1,0:T(1,128)} %pc_hbm.1, bf16[1,64,1024]{2,1,0:T(8,128)(2,1)} %row_ref.1, ...), custom_call_target="tpu_custom_call" | custom-call | tf_op jit(solution)/shard_map/pallas_call | solution.py:164
  31.8 0.0 copy-start
  31.8 0.6 %copy-done = bf16[256,256]{1,0:T(8,128)(2,1)} copy-done((bf16[256,256]{1,0:T(8,128)(2,1)}, bf16[256,256]{1,0:T(8,128)(2,1)S(1)}, u32[]{:S(2)}) %copy-start) | copy-done | bytes 131096
  32.5 0.0 copy-start.1
  32.5 0.6 %copy-done.1 = bf16[1,64,1024]{2,1,0:T(8,128)(2,1)} copy-done((bf16[1,64,1024]{2,1,0:T(8,128)(2,1)}, bf16[1,64,1024]{2,1,0:T(8,128)(2,1)S(1)}, u32[]{:S(2)}) %copy-start.1) | copy-done | bytes 131096
  33.1 0.0 copy-start.2
  33.1 0.7 %copy-done.2 = bf16[1,64,1024]{2,1,0:T(8,128)(2,1)} copy-done((bf16[1,64,1024]{2,1,0:T(8,128)(2,1)}, bf16[1,64,1024]{2,1,0:T(8,128)(2,1)S(1)}, u32[]{:S(2)}) %copy-start.2) | copy-done | bytes 131096
  33.7 1.8 %shard_map.86 = (bf16[256,256]{1,0:T(8,128)(2,1)}, bf16[1,64,1024]{2,1,0:T(8,128)(2,1)}, bf16[1,64,1024]{2,1,0:T(8,128)(2,1)}) custom-call(bf16[256,256]{1,0:T(8,128)(2,1)} %copy-done, bf16[1,64,1024]{2,1,0:T(8,128)(2,1)} %copy-done.1, bf16[1,64,1024]{2,1,0:T(8,128)(2,1)} %copy-done.2), custom_call_target="tpu_custom_call" | custom-call | tf_op jit(solution)/shard_map/pallas_call | solution.py:197
Async XLA Ops:
  31.8 0.6 %copy-start = (bf16[256,256]{1,0:T(8,128)(2,1)}, bf16[256,256]{1,0:T(8,128)(2,1)S(1)}, u32[]{:S(2)}) copy-start(bf16[256,256]{1,0:T(8,128)(2,1)S(1)} %get-tuple-element.6.refs_0_) | copy-start | bytes 393220
  32.5 0.6 %copy-start.1 = (bf16[1,64,1024]{2,1,0:T(8,128)(2,1)}, bf16[1,64,1024]{2,1,0:T(8,128)(2,1)S(1)}, u32[]{:S(2)}) copy-start(bf16[1,64,1024]{2,1,0:T(8,128)(2,1)S(1)} %get-tuple-element.7.refs_1_) | copy-start | bytes 393220
  33.1 0.7 %copy-start.2 = (bf16[1,64,1024]{2,1,0:T(8,128)(2,1)}, bf16[1,64,1024]{2,1,0:T(8,128)(2,1)S(1)}, u32[]{:S(2)}) copy-start(bf16[1,64,1024]{2,1,0:T(8,128)(2,1)S(1)} %get-tuple-element.8.refs_2_) | copy-start | bytes 393220

commit v3 on v2

--- a/solution.py
+++ b/solution.py
@@ -8,13 +8,7 @@
 from jax.sharding import PartitionSpec as P
 
 NT = (((1,), (1,)), ((), ()))
-
-
-def nearest(me, n, step):
-    inner = jnp.minimum(me, n - 1 - me)
-    both = (step + 1) // 2 * (2 * (step % 2) - 1)
-    one = (step - inner) * jnp.where(2 * me < n, 1, -1)
-    return me + jnp.where(step <= 2 * inner, both, one)
+CHUNKS = 1
 
 
 def kernel(
@@ -49,23 +43,46 @@
             src_ref=src, dst_ref=dst, send_sem=send, recv_sem=recv, device_id=where, device_id_type=pl.DeviceIdType.MESH
         )
 
-    def row_copy(k, slot):
-        return remote(row_ref.at[0], rows.at[slot], row_send.at[k], row_recv.at[slot], (g, r, lax.rem(c + k, nc)))
-
-    def col_copy(peer, slot):
-        return remote(col_ref.at[0], cols.at[slot], col_send.at[peer], col_recv.at[slot], (g, peer, c))
-
-    def cp_copy(peer, slot):
-        return remote(cp.at[peer], cp_in.at[slot], cp_send.at[peer], cp_recv.at[slot], (g, peer, c))
-
-    def rp_copy(peer, slot):
-        return remote(rp.at[peer], rp_in.at[slot], rp_send.at[peer], rp_recv.at[slot], (g, r, peer))
-
+    half = nr // 2 if nr % 2 == 0 else nr
+    base = r // half * half
+    across = lax.rem(r + half, nr)
+    near = [base + lax.rem(r - base + k, half) for k in range(1, half)]
+    step = cs // CHUNKS
+
+    def other_half(s):
+        return lax.rem(s + half, nr)
+
+    def mate(d):
+        return d + 1 - 2 * (d % 2)
+
+    def chunk(ref, h):
+        return ref.at[pl.ds(h * step, step)]
+
+    def row_copy(to, slot, own):
+        src = row_ref.at[0] if own else rows.at[slot]
+        return remote(src, rows.at[slot], row_send.at[to if own else mate(slot)], row_recv.at[slot], (g, r, to))
+
+    def col_copy(to, slot, h, own):
+        src = col_ref.at[0] if own else cols.at[slot]
+        send = col_send.at[to if own else other_half(to), h]
+        return remote(chunk(src, h), chunk(cols.at[slot], h), send, col_recv.at[slot, h], (g, to, c))
+
+    def cp_copy(to, slot, h):
+        return remote(chunk(cp.at[to], h), chunk(cp_in.at[slot], h), cp_send.at[to, h], cp_recv.at[slot, h], (g, to, c))
+
+    def rp_copy(to, slot):
+        return remote(rp.at[to], rp_in.at[slot], rp_send.at[to], rp_recv.at[slot], (g, r, to))
+
+    chips = [lax.rem(c + 2 * k, nc) for k in range(1, nc // 2)]
     pl.semaphore_wait(barrier, nr + nc - 2)
-    for k in range(1, nr):
-        col_copy(nearest(r, nr, k), r).start()
-    for k in range(1, nc):
-        row_copy(k, c).start()
+    if half < nr:
+        for h in range(CHUNKS):
+            col_copy(across, r, h, True).start()
+    for to in [*chips, mate(c)]:
+        row_copy(to, c, True).start()
+    for h in range(CHUNKS):
+        for to in near:
+            col_copy(to, r, h, True).start()
 
     for copy in small:
         copy.wait()
@@ -78,31 +95,63 @@
 
     own_row.wait()
     own_col.wait()
-    for k in range(1, nc):
-        row_copy(k, lax.rem(c + k, nc)).wait_recv()
-
-    def block(s):
-        at = pl.ds(pl.multiple_of(s * cs, cs), cs)
+    for s in chips:
+        row_copy(c, s, True).wait_recv()
+        row_copy(mate(c), s, False).start()
+
+    def block(s, h):
+        first = s * cs + h * step
+        at = pl.ds(pl.multiple_of(first, step), step)
         row_all = rows[...].reshape(rows_tile, depth)
-        scores = factor * lax.dot_general(cols[s], row_all, NT, preferred_element_type=jnp.float32) + offset
+        part = cols[s, pl.ds(h * step, step)]
+        scores = factor * lax.dot_general(part, row_all, NT, preferred_element_type=jnp.float32) + offset
         lt[at, :] = scores
         grad = (jax.nn.sigmoid(scores) - labels[at, :]).astype(jnp.bfloat16)
         gt[at, :] = grad
         return jnp.dot(grad, row_all, preferred_element_type=jnp.float32).astype(jnp.bfloat16)
 
-    cp_in[r] = block(r)
-
-    def arrived(k):
-        s = nearest(r, nr, k)
-        col_copy(s, s).wait_recv()
-        cp[s] = block(s)
-        cp_copy(s, r).start()
-
-    if nr <= 4:
-        for k in range(1, nr):
-            arrived(k)
-    else:
-        pl.loop(1, nr)(arrived)
+    def arrived(s, h):
+        cp[s, pl.ds(h * step, step)] = block(s, h)
+        cp_copy(s, r, h).start()
+
+    def have_rows():
+        for s in [c, *chips]:
+            row_copy(c, mate(s), True).wait_recv()
+
+    for h in range(CHUNKS):
+        if half < nr:
+            col_copy(r, across, h, True).wait_recv()
+            for to in near:
+                col_copy(to, across, h, False).start()
+        if h == 0:
+            have_rows()
+        if half < nr:
+            arrived(across, h)
+
+    def from_near(k):
+        s = base + lax.rem(r - base + k, half)
+        for h in range(CHUNKS):
+            col_copy(r, s, h, True).wait_recv()
+            arrived(s, h)
+
+    def from_far(k):
+        s = other_half(base + lax.rem(r - base + k, half))
+        for h in range(CHUNKS):
+            col_copy(r, s, h, True).wait_recv()
+            arrived(s, h)
+
+    def in_turn(body):
+        if half <= 2:
+            for k in range(1, half):
+                body(k)
+        else:
+            pl.loop(1, half)(body)
+
+    in_turn(from_near)
+    for h in range(CHUNKS):
+        cp_in[r, pl.ds(h * step, step)] = block(r, h)
+    if half < nr:
+        in_turn(from_far)
 
     cols_all = cols[...].reshape(cols_tile, depth)
     grad = gt[...].T
@@ -119,32 +168,31 @@
             add += parts[s].astype(jnp.float32)
         return (factor * add).astype(jnp.bfloat16)
 
-    for k in range(1, nr):
-        s = nearest(r, nr, k)
-        cp_copy(s, s).wait_recv()
-    col_out[0] = total(cp_in, nr)
     for k in range(1, nc):
         s = lax.rem(c + k, nc)
         rp_copy(s, s).wait_recv()
     row_out[0] = total(rp_in, nc)
-
     for k in range(1, nr):
-        s = nearest(r, nr, k)
-        col_copy(s, r).wait_send()
-        cp_copy(s, r).wait_send()
-    for k in range(1, nc):
-        row_copy(k, c).wait_send()
+        s = lax.rem(r + k, nr)
+        for h in range(CHUNKS):
+            cp_copy(s, s, h).wait_recv()
+    col_out[0] = total(cp_in, nr)
+
+    for h in range(CHUNKS):
+        if half < nr:
+            col_copy(across, r, h, True).wait_send()
+        for to in near:
+            col_copy(to, r, h, True).wait_send()
+            if half < nr:
+                col_copy(to, across, h, False).wait_send()
+        for k in range(1, nr):
+            cp_copy(lax.rem(r + k, nr), r, h).wait_send()
+    for to in [*chips, mate(c)]:
+        row_copy(to, c, True).wait_send()
+    for s in chips:
+        row_copy(mate(c), s, False).wait_send()
+    for k in range(1, nc):
         rp_copy(lax.rem(c + k, nc), c).wait_send()
-
-
-def write_out(*refs):
-    sems = refs[-1]
-    held, out = refs[:3], refs[3:6]
-    copies = [pltpu.make_async_copy(src, dst, sems.at[i]) for i, (src, dst) in enumerate(zip(held, out))]
-    for copy in copies:
-        copy.start()
-    for copy in copies:
-        copy.wait()
 
 
 def local(nr, nc, row_embed, col_embed, pos_rows, pos_cols, logit_scale, logit_bias):
@@ -161,7 +209,7 @@
     )
     operands = (pos_rows, pos_cols, row_embed, col_embed)
     pinned = [pltpu.with_memory_space_constraint(x, pltpu.HBM) for x in operands]
-    held = pl.pallas_call(
+    return pl.pallas_call(
         functools.partial(kernel, nr, nc),
         out_shape=shapes,
         in_specs=[hbm] * 6,
@@ -183,10 +231,10 @@
             dma((6,)),
             dma((nc,)),
             dma((nc,)),
-            dma((nr,)),
-            dma((nr,)),
-            dma((nr,)),
-            dma((nr,)),
+            dma((nr, CHUNKS)),
+            dma((nr, CHUNKS)),
+            dma((nr, CHUNKS)),
+            dma((nr, CHUNKS)),
             dma((nc,)),
             dma((nc,)),
         ],
@@ -194,13 +242,6 @@
             collective_id=0, has_side_effects=True, vmem_limit_bytes=50 * 1024 * 1024
         ),
     )(logit_scale, logit_bias, *pinned)
-    return pl.pallas_call(
-        write_out,
-        out_shape=shapes,
-        in_specs=[vmem] * 3,
-        out_specs=(hbm,) * 3,
-        scratch_shapes=[dma((3,))],
-    )(*held)
 
 
 def solution(mesh):

time: 35.7 us -> 29.7 us (0.83)
  Pallas kernels: 31.7 us -> 25.6 us
    pallas_call x1, Pallas kernels: 29.9 us -> 25.6 us  [local(): pl.pallas_call(functools.partial(kernel, nr, nc), out_shape=shapes, in_sp...]
    pallas_call x1 -> x0, Pallas kernels: 1.79 us -> none  [local(): pl.pallas_call(write_out, out_shape=shapes, in_specs=[vmem] * 3, out_spec...]
    unnamed x6 -> x3, local copies, waits for them, and re-layouts: 1.92 us -> 1.97 us
where the time goes in v3:
time: 29.7 us; the launch traced here: 29.5 us
  Pallas kernels  25.6 us (86%)
  local copies, waits for them, and re-layouts  1.97 us (7%)
  between operations  1.93 us (6%)
    pallas_call x1, Pallas kernels, local(): pl.pallas_call(functools.partial(kernel, nr, nc), out_shape=shapes, in_sp...  25.6 us
    unnamed x3, local copies, waits for them, and re-layouts  1.97 us

profile of v3, /device:TPU:0, one launch (start us, length us, event | category | flops | bytes accessed | tf_op | source)
XLA Modules:
  0.0 29.5 jit_solution(3816703495302697676)
XLA Ops:
  1.9 25.6 %shard_map.85 = (bf16[256,256]{1,0:T(8,128)(2,1)S(1)}, bf16[1,64,1024]{2,1,0:T(8,128)(2,1)S(1)}, bf16[1,64,1024]{2,1,0:T(8,128)(2,1)S(1)}) custom-call(f32[1]{0:T(128)S(6)} %copy.12.scale_hbm, f32[1]{0:T(128)S(6)} %copy.13.bias_hbm, s32[1,1,256]{2,1,0:T(1,128)} %pr_hbm.1, s32[1,1,256]{2,1,0:T(1,128)} %pc_hbm.1, bf16[1,64,1024]{2,1,0:T(8,128)(2,1)} %row_ref.1, ...), custom_call_target="tpu_custom_call" | custom-call | tf_op jit(solution)/shard_map/pallas_call | solution.py:212
  27.6 0.7 %copy.14 = bf16[256,256]{1,0:T(8,128)(2,1)} copy(bf16[256,256]{1,0:T(8,128)(2,1)S(1)} %get-tuple-element.6) | data formatting | bytes 262144
  28.2 0.7 %copy.15 = bf16[1,64,1024]{2,1,0:T(8,128)(2,1)} copy(bf16[1,64,1024]{2,1,0:T(8,128)(2,1)S(1)} %get-tuple-element.7) | data formatting | bytes 262144
  28.9 0.7 %copy.16 = bf16[1,64,1024]{2,1,0:T(8,128)(2,1)} copy(bf16[1,64,1024]{2,1,0:T(8,128)(2,1)S(1)} %get-tuple-element.8) | data formatting | bytes 262144

commit v4 on v3

--- a/solution.py
+++ b/solution.py
@@ -8,12 +8,12 @@
 from jax.sharding import PartitionSpec as P
 
 NT = (((1,), (1,)), ((), ()))
-CHUNKS = 1
+CHUNKS = 2
 
 
 def kernel(
     nr, nc, scale_hbm, bias_hbm, pr_hbm, pc_hbm, row_ref, col_ref,
-    logit_out, row_out, col_out,
+    logit_out, grads_out,
     scale_ref, bias_ref, pr_ref, pc_ref, rows, cols, labels, lt, gt, cp, cp_in, rp, rp_in,
     own_sem, row_send, row_recv, col_send, col_recv, cp_send, cp_recv, rp_send, rp_recv,
 ):
@@ -22,11 +22,19 @@
     depth = row_ref.shape[2]
     rows_tile, cols_tile = rs * nc, cs * nr
 
+    half = nr // 2 if nr % 2 == 0 else nr
+    base = r // half * half
+    across = lax.rem(r + half, nr)
+    near = [base + lax.rem(r - base + k, half) for k in range(1, half)]
+    chips = [lax.rem(c + 2 * k, nc) for k in range(1, nc // 2)]
+
+    def mate(d):
+        return d + 1 - 2 * (d % 2)
+
+    first = [(g, lax.rem(r + k, nr), c) for k in range(1, nr)] + [(g, r, lax.rem(c + k, nc)) for k in range(1, nc)]
     barrier = pltpu.get_barrier_semaphore()
-    for k in range(1, nr):
-        pl.semaphore_signal(barrier, inc=1, device_id=(g, lax.rem(r + k, nr), c), device_id_type=pl.DeviceIdType.MESH)
-    for k in range(1, nc):
-        pl.semaphore_signal(barrier, inc=1, device_id=(g, r, lax.rem(c + k, nc)), device_id_type=pl.DeviceIdType.MESH)
+    for where in first:
+        pl.semaphore_signal(barrier, inc=1, device_id=where, device_id_type=pl.DeviceIdType.MESH)
     own_row = pltpu.make_async_copy(row_ref.at[0], rows.at[c], own_sem.at[0])
     own_col = pltpu.make_async_copy(col_ref.at[0], cols.at[r], own_sem.at[1])
     small = [
@@ -43,17 +51,10 @@
             src_ref=src, dst_ref=dst, send_sem=send, recv_sem=recv, device_id=where, device_id_type=pl.DeviceIdType.MESH
         )
 
-    half = nr // 2 if nr % 2 == 0 else nr
-    base = r // half * half
-    across = lax.rem(r + half, nr)
-    near = [base + lax.rem(r - base + k, half) for k in range(1, half)]
     step = cs // CHUNKS
 
     def other_half(s):
         return lax.rem(s + half, nr)
-
-    def mate(d):
-        return d + 1 - 2 * (d % 2)
 
     def chunk(ref, h):
         return ref.at[pl.ds(h * step, step)]
@@ -67,14 +68,13 @@
         send = col_send.at[to if own else other_half(to), h]
         return remote(chunk(src, h), chunk(cols.at[slot], h), send, col_recv.at[slot, h], (g, to, c))
 
-    def cp_copy(to, slot, h):
-        return remote(chunk(cp.at[to], h), chunk(cp_in.at[slot], h), cp_send.at[to, h], cp_recv.at[slot, h], (g, to, c))
+    def cp_copy(to, slot):
+        return remote(cp.at[to], cp_in.at[slot], cp_send.at[to, 0], cp_recv.at[slot, 0], (g, to, c))
 
     def rp_copy(to, slot):
         return remote(rp.at[to], rp_in.at[slot], rp_send.at[to], rp_recv.at[slot], (g, r, to))
 
-    chips = [lax.rem(c + 2 * k, nc) for k in range(1, nc // 2)]
-    pl.semaphore_wait(barrier, nr + nc - 2)
+    pl.semaphore_wait(barrier, len(first))
     if half < nr:
         for h in range(CHUNKS):
             col_copy(across, r, h, True).start()
@@ -99,46 +99,38 @@
         row_copy(c, s, True).wait_recv()
         row_copy(mate(c), s, False).start()
 
-    def block(s, h):
-        first = s * cs + h * step
-        at = pl.ds(pl.multiple_of(first, step), step)
+    def block(s):
+        at = pl.ds(pl.multiple_of(s * cs, cs), cs)
         row_all = rows[...].reshape(rows_tile, depth)
-        part = cols[s, pl.ds(h * step, step)]
-        scores = factor * lax.dot_general(part, row_all, NT, preferred_element_type=jnp.float32) + offset
+        scores = factor * lax.dot_general(cols[s], row_all, NT, preferred_element_type=jnp.float32) + offset
         lt[at, :] = scores
         grad = (jax.nn.sigmoid(scores) - labels[at, :]).astype(jnp.bfloat16)
         gt[at, :] = grad
         return jnp.dot(grad, row_all, preferred_element_type=jnp.float32).astype(jnp.bfloat16)
 
-    def arrived(s, h):
-        cp[s, pl.ds(h * step, step)] = block(s, h)
-        cp_copy(s, r, h).start()
-
-    def have_rows():
-        for s in [c, *chips]:
-            row_copy(c, mate(s), True).wait_recv()
-
-    for h in range(CHUNKS):
-        if half < nr:
+    if half < nr:
+        for h in range(CHUNKS):
             col_copy(r, across, h, True).wait_recv()
             for to in near:
                 col_copy(to, across, h, False).start()
-        if h == 0:
-            have_rows()
-        if half < nr:
-            arrived(across, h)
+    for s in [c, *chips]:
+        row_copy(c, mate(s), True).wait_recv()
+    if half < nr:
+        cp[across] = block(across)
+        cp_copy(across, r).start()
 
     def from_near(k):
         s = base + lax.rem(r - base + k, half)
         for h in range(CHUNKS):
             col_copy(r, s, h, True).wait_recv()
-            arrived(s, h)
+        cp[s] = block(s)
 
     def from_far(k):
         s = other_half(base + lax.rem(r - base + k, half))
         for h in range(CHUNKS):
             col_copy(r, s, h, True).wait_recv()
-            arrived(s, h)
+        cp[s] = block(s)
+        cp_copy(s, r).start()
 
     def in_turn(body):
         if half <= 2:
@@ -148,10 +140,11 @@
             pl.loop(1, half)(body)
 
     in_turn(from_near)
-    for h in range(CHUNKS):
-        cp_in[r, pl.ds(h * step, step)] = block(r, h)
+    cp_in[r] = block(r)
     if half < nr:
         in_turn(from_far)
+    for to in near:
+        cp_copy(to, r).start()
 
     cols_all = cols[...].reshape(cols_tile, depth)
     grad = gt[...].T
@@ -171,12 +164,11 @@
     for k in range(1, nc):
         s = lax.rem(c + k, nc)
         rp_copy(s, s).wait_recv()
-    row_out[0] = total(rp_in, nc)
+    grads_out[pl.ds(0, rs)] = total(rp_in, nc)
     for k in range(1, nr):
         s = lax.rem(r + k, nr)
-        for h in range(CHUNKS):
-            cp_copy(s, s, h).wait_recv()
-    col_out[0] = total(cp_in, nr)
+        cp_copy(s, s).wait_recv()
+    grads_out[pl.ds(rs, cs)] = total(cp_in, nr)
 
     for h in range(CHUNKS):
         if half < nr:
@@ -185,8 +177,8 @@
             col_copy(to, r, h, True).wait_send()
             if half < nr:
                 col_copy(to, across, h, False).wait_send()
-        for k in range(1, nr):
-            cp_copy(lax.rem(r + k, nr), r, h).wait_send()
+    for k in range(1, nr):
+        cp_copy(lax.rem(r + k, nr), r).wait_send()
     for to in [*chips, mate(c)]:
         row_copy(to, c, True).wait_send()
     for s in chips:
@@ -204,16 +196,15 @@
     dma = pltpu.SemaphoreType.DMA
     shapes = (
         jax.ShapeDtypeStruct((rows_tile, cols_tile), bf16),
-        jax.ShapeDtypeStruct((1, rs, depth), bf16),
-        jax.ShapeDtypeStruct((1, cs, depth), bf16),
+        jax.ShapeDtypeStruct((rs + cs, depth), bf16),
     )
     operands = (pos_rows, pos_cols, row_embed, col_embed)
     pinned = [pltpu.with_memory_space_constraint(x, pltpu.HBM) for x in operands]
-    return pl.pallas_call(
+    logits, grads = pl.pallas_call(
         functools.partial(kernel, nr, nc),
         out_shape=shapes,
         in_specs=[hbm] * 6,
-        out_specs=(vmem,) * 3,
+        out_specs=(vmem,) * 2,
         scratch_shapes=[
             pltpu.SMEM((1,), f32),
             pltpu.SMEM((1,), f32),
@@ -242,6 +233,7 @@
             collective_id=0, has_side_effects=True, vmem_limit_bytes=50 * 1024 * 1024
         ),
     )(logit_scale, logit_bias, *pinned)
+    return logits, grads[None, :rs], grads[None, rs:]
 
 
 def solution(mesh):

time: 29.7 us -> 29 us (0.976); the launches traced: 29.5 us -> 28.5 us
  local copies, waits for them, and re-layouts: 1.97 us -> 1.37 us
  Pallas kernels: 25.6 us -> 25.2 us
    unnamed x3 -> x1, local copies, waits for them, and re-layouts: 1.97 us -> 0.65 us
    broadcast_in_dim x0 -> x1, local copies, waits for them, and re-layouts: none -> 0.72 us  [local(): return (logits, grads[None, :rs], grads[None, rs:])]
    pallas_call x1, Pallas kernels: 25.6 us -> 25.2 us  [local(): pl.pallas_call(functools.partial(kernel, nr, nc), out_shape=shapes, in_sp...]
where the time goes in v4:
time: 29 us; the launch traced here: 28.5 us
  Pallas kernels  25.2 us (87%)
  between operations  1.93 us (7%)
  local copies, waits for them, and re-layouts  1.37 us (5%)
    pallas_call x1, Pallas kernels, local(): pl.pallas_call(functools.partial(kernel, nr, nc), out_shape=shapes, in_sp...  25.2 us
    broadcast_in_dim x1, local copies, waits for them, and re-layouts, local(): return (logits, grads[None, :rs], grads[None, rs:])  0.72 us
    unnamed x1, local copies, waits for them, and re-layouts  0.65 us

profile of v4, /device:TPU:0, one launch (start us, length us, event | category | flops | bytes accessed | tf_op | source)
XLA Modules:
  0.0 28.5 jit_solution(4411960401011923643)
XLA Ops:
  1.9 25.2 %shard_map.85 = (bf16[256,256]{1,0:T(8,128)(2,1)S(1)}, bf16[128,1024]{1,0:T(8,128)(2,1)S(1)}) custom-call(f32[1]{0:T(128)S(6)} %copy.10.scale_hbm, f32[1]{0:T(128)S(6)} %copy.11.bias_hbm, s32[1,1,256]{2,1,0:T(1,128)} %pr_hbm.1, s32[1,1,256]{2,1,0:T(1,128)} %pc_hbm.1, bf16[1,64,1024]{2,1,0:T(8,128)(2,1)} %row_ref.1, bf16[1,64,1024]{2,1,0:T(8,128)(2,1)} %col_ref.1), custom_call_target="tpu_custom_call" | custom-call | tf_op jit(solution)/shard_map/pallas_call | solution.py:203
  27.1 0.7 %slice_bitcast_fusion = (bf16[1,64,1024]{2,1,0:T(8,128)(2,1)}, bf16[1,64,1024]{2,1,0:T(8,128)(2,1)}) fusion(bf16[128,1024]{1,0:T(8,128)(2,1)S(1)} %get-tuple-element.6), kind=kLoop, calls=%fused_computation | loop fusion | bytes 524288 | tf_op jit(solution)/shard_map/broadcast_in_dim | solution.py:236
  27.8 0.7 %copy.12 = bf16[256,256]{1,0:T(8,128)(2,1)} copy(bf16[256,256]{1,0:T(8,128)(2,1)S(1)} %get-tuple-element.12) | data formatting | bytes 262144

commit v5 on v4

--- a/solution.py
+++ b/solution.py
@@ -8,7 +8,7 @@
 from jax.sharding import PartitionSpec as P
 
 NT = (((1,), (1,)), ((), ()))
-CHUNKS = 2
+CHUNKS = 1
 
 
 def kernel(
@@ -24,7 +24,7 @@
 
     half = nr // 2 if nr % 2 == 0 else nr
     base = r // half * half
-    across = lax.rem(r + half, nr)
+    across = nr - 1 - r
     near = [base + lax.rem(r - base + k, half) for k in range(1, half)]
     chips = [lax.rem(c + 2 * k, nc) for k in range(1, nc // 2)]
 
@@ -54,7 +54,7 @@
     step = cs // CHUNKS
 
     def other_half(s):
-        return lax.rem(s + half, nr)
+        return nr - 1 - s
 
     def chunk(ref, h):
         return ref.at[pl.ds(h * step, step)]

time: 29 us -> 28.9 us (level); the launches traced: 28.5 us -> 28.7 us
  no operation moved by 1% of the time
where the time goes in v5:
time: 28.9 us; the launch traced here: 28.7 us
  Pallas kernels  25.4 us (88%)
  between operations  1.93 us (7%)
  local copies, waits for them, and re-layouts  1.37 us (5%)
    pallas_call x1, Pallas kernels, local(): pl.pallas_call(functools.partial(kernel, nr, nc), out_shape=shapes, in_sp...  25.4 us
    broadcast_in_dim x1, local copies, waits for them, and re-layouts, local(): return (logits, grads[None, :rs], grads[None, rs:])  0.72 us
    unnamed x1, local copies, waits for them, and re-layouts  0.65 us

profile of v5, /device:TPU:0, one launch (start us, length us, event | category | flops | bytes accessed | tf_op | source)
XLA Modules:
  0.0 28.7 jit_solution(7096290821984459442)
XLA Ops:
  1.9 25.4 %shard_map.85 = (bf16[256,256]{1,0:T(8,128)(2,1)S(1)}, bf16[128,1024]{1,0:T(8,128)(2,1)S(1)}) custom-call(f32[1]{0:T(128)S(6)} %copy.10.scale_hbm, f32[1]{0:T(128)S(6)} %copy.11.bias_hbm, s32[1,1,256]{2,1,0:T(1,128)} %pr_hbm.1, s32[1,1,256]{2,1,0:T(1,128)} %pc_hbm.1, bf16[1,64,1024]{2,1,0:T(8,128)(2,1)} %row_ref.1, bf16[1,64,1024]{2,1,0:T(8,128)(2,1)} %col_ref.1), custom_call_target="tpu_custom_call" | custom-call | tf_op jit(solution)/shard_map/pallas_call | solution.py:203
  27.3 0.7 %slice_bitcast_fusion = (bf16[1,64,1024]{2,1,0:T(8,128)(2,1)}, bf16[1,64,1024]{2,1,0:T(8,128)(2,1)}) fusion(bf16[128,1024]{1,0:T(8,128)(2,1)S(1)} %get-tuple-element.6), kind=kLoop, calls=%fused_computation | loop fusion | bytes 524288 | tf_op jit(solution)/shard_map/broadcast_in_dim | solution.py:236
  28.0 0.7 %copy.12 = bf16[256,256]{1,0:T(8,128)(2,1)} copy(bf16[256,256]{1,0:T(8,128)(2,1)S(1)} %get-tuple-element.12) | data formatting | bytes 262144
